TPU v7x, 32 devices: a whole 2x2x4 slice. The times are simulated.
32 devices in a mesh: gx: 2 (over y), gy: 4 (over z), gz: 4 (over x, core).
Axes of the slice: x: 2, y: 2, z: 4, core: 2. Of those that a mesh axis runs over, the one named last changes fastest.
Arguments:
- shape_coef: float32 [2, 4, 4, 4, 3, 169], P('gx', 'gy', 'gz')
- density_coef: float32 [2, 4, 4, 4, 3, 169], P('gx', 'gy', 'gz'), may hold values from -1.8 to 1.8
- pair_count: int32 [2, 4, 4], P('gx', 'gy', 'gz'), may hold values from 4 to 12, as said below
- pair_slots: int32 [2, 4, 4, 12, 2], P('gx', 'gy', 'gz'), may hold values from 0 to 107, as said below
Outputs:
- vel_coef: float32 [2, 4, 4, 4, 3, 169], P('gx', 'gy', 'gz')
Inputs may be any that keep to these rules, and one draw needn't show every extreme that they name: `pair_count`: each device owns from 4 to 12 close pairs; some device owns exactly 12. `pair_slots`: an entry names a vesicle of the owner or of a device next to it (diagonals included) that exists in the grid; the first entry of every slot names a vesicle of the owner; the two vesicles of a slot differ; every vesicle is the first of one of its own device's first 4 slots; slots at or beyond the owner's pair_count are not read.
All inputs are finite; a program needn't handle non-finite values.
Results may differ from a plain program's by a relative error of at most 0.0003.
Values sent between devices are 32-bit elements; how exact they have to be, the bound alone decides.
A program may use at most 64 MiB of HBM per device.

v0:
```python
import functools
import itertools
import math

import jax
import jax.numpy as jnp
import numpy as np
from jax import lax
from jax.experimental import pallas as pl
from jax.experimental.pallas import tpu as pltpu
from jax.sharding import PartitionSpec as P

P_SIZE = 12
Q = 24


blob_radius = 0.25

def gauss_nodes(node_count):
    numbers = np.arange(1, node_count + 1)
    cosine = np.cos(np.pi * (numbers - 0.25) / (node_count + 0.5))

    def legendre_pair(points):
        legendre_prev = np.ones(points.shape)
        legendre_next = np.array(points)
        for degree in range(2, node_count + 1):
            legendre_prev, legendre_next = (
                legendre_next,
                ((2.0 * degree - 1.0) * points * legendre_next - (degree - 1.0) * legendre_prev)
                / degree,
            )
        slope = node_count * (points * legendre_next - legendre_prev) / (points * points - 1.0)
        return (legendre_next, slope)

    for newton_step in range(100):
        value_now, slope = legendre_pair(cosine)
        cosine = cosine - value_now / slope
    value_now, slope = legendre_pair(cosine)
    weights = 2.0 / ((1.0 - cosine * cosine) * slope * slope)
    return (np.array(cosine[::-1]), np.array(weights[::-1]))


def harmonic_table(top_degree, latitudes, longitudes):
    cosine, gauss_weight = gauss_nodes(latitudes)
    sine_theta = np.sqrt(1.0 - cosine * cosine)
    angles = 2.0 * np.pi * np.arange(longitudes) / longitudes
    legendre = np.zeros((top_degree + 1, top_degree + 1, latitudes))
    legendre[0, 0] = np.sqrt(0.25 / np.pi)
    for degree_m in range(1, top_degree + 1):
        legendre[degree_m, degree_m] = (
            np.sqrt((2.0 * degree_m + 1.0) / (2.0 * degree_m))
            * sine_theta
            * legendre[degree_m - 1, degree_m - 1]
        )
    for degree_m in range(top_degree + 1):
        if degree_m + 1 <= top_degree:
            legendre[degree_m + 1, degree_m] = (
                np.sqrt(2.0 * degree_m + 3.0) * cosine * legendre[degree_m, degree_m]
            )
        for degree_l in range(degree_m + 2, top_degree + 1):
            factor = np.sqrt(
                (4.0 * degree_l * degree_l - 1.0) / (degree_l * degree_l - degree_m * degree_m)
            )
            lagged = np.sqrt(
                ((degree_l - 1.0) * (degree_l - 1.0) - degree_m * degree_m)
                / (4.0 * (degree_l - 1.0) * (degree_l - 1.0) - 1.0)
            )
            legendre[degree_l, degree_m] = factor * (
                cosine * legendre[degree_l - 1, degree_m]
                - lagged * legendre[degree_l - 2, degree_m]
            )
    table_rows = []
    for degree_l in range(top_degree + 1):
        for signed in range(-degree_l, degree_l + 1):
            polar_part = legendre[degree_l, abs(signed)][:, None]
            if signed > 0:
                azimuth = np.sqrt(2.0) * np.cos(signed * angles)
            elif signed < 0:
                azimuth = np.sqrt(2.0) * np.sin(-signed * angles)
            else:
                azimuth = np.ones(longitudes)
            table_rows.append((polar_part * azimuth[None, :]).reshape(-1))
    synthesis = np.stack(table_rows)
    weights = np.repeat(gauss_weight, longitudes) * (2.0 * np.pi / longitudes)
    return (synthesis, weights)

AXES = ("gx", "gy", "gz")
OFFSETS = list(itertools.product((-1, 0, 1), repeat=3))
HEAD = 128
TAIL = 41
MESSAGE = 40
T_PAD = 384
T_ROWS = 352
S_PAD = 1280
CHUNK = 1280
COLS = 16


def split_table(table):
    high = table.astype(np.float32).astype(jnp.bfloat16)
    low = (table - high.astype(np.float64)).astype(jnp.bfloat16)
    pad = np.zeros((512 - 3 * table.shape[0], table.shape[1]), jnp.bfloat16)
    return np.concatenate(
        [high[:HEAD], low[:HEAD], high[:HEAD], high[HEAD:], low[HEAD:], high[HEAD:], pad]
    )


def grid_tables():
    target_synth, target_weight = harmonic_table(P_SIZE, P_SIZE + 1, 2 * (P_SIZE + 1))
    upsample_synth, upsample_weight = harmonic_table(P_SIZE, Q + 1, 2 * (Q + 1))
    targets, sources = target_synth.shape[1], upsample_synth.shape[1]
    target_wide = np.pad(target_synth, ((0, 0), (0, T_PAD - targets)))
    source_wide = np.pad(upsample_synth, ((0, 0), (0, S_PAD - sources)))
    weight_rows = np.pad(upsample_weight, (0, S_PAD - sources)).reshape(-1, 256)
    weight_rows = np.pad(weight_rows, ((0, 8 - weight_rows.shape[0]), (0, 0)))
    analysis = np.pad(
        (target_synth * target_weight[None, :]).T,
        ((0, T_PAD - targets), (0, 256 - target_synth.shape[0])),
    )
    return (
        jnp.asarray(split_table(source_wide)),
        jnp.asarray(np.ascontiguousarray(split_table(target_wide).T)),
        jnp.asarray(np.concatenate([analysis, weight_rows]), dtype=jnp.float32),
    )


def halo_kernel(
    sizes, shape_ref, density_ref, slots_ref, count_ref, out_ref, names_ref,
    own_ref, tail_ref, send_sem, recv_sem,
):
    here = [lax.axis_index(axis) for axis in AXES]

    def place(offset):
        there = [h + o for h, o in zip(here, offset)]
        exists = None
        for spot, o, size in zip(there, offset, sizes):
            if o:
                inside = (spot >= 0) & (spot < size)
                exists = inside if exists is None else exists & inside
        return tuple(there), exists

    barrier = pltpu.get_barrier_semaphore()
    around = 1
    for h, size in zip(here, sizes):
        around = around * (1 + (h > 0).astype(jnp.int32) + (h < size - 1).astype(jnp.int32))
    for offset in OFFSETS:
        if any(offset):
            there, exists = place(offset)

            @pl.when(exists)
            def _():
                pl.semaphore_signal(
                    barrier, inc=1, device_id=there, device_id_type=pl.DeviceIdType.MESH
                )

    own_ref[32:MESSAGE, :] = jnp.zeros((MESSAGE - 32, HEAD), jnp.float32)
    tail_ref[...] = jnp.zeros(tail_ref.shape, jnp.float32)
    for start, source in ((0, shape_ref), (12, density_ref)):
        for i in range(3):
            rows = slice(start + 4 * i, start + 4 * i + 4)
            own_ref[rows, :] = source[i, :, 0:HEAD]
            tail_ref[rows, 0:TAIL] = source[i, :, HEAD : HEAD + TAIL]
    own_ref[24:32, :] = (
        tail_ref[0:8, :]
        + pltpu.roll(tail_ref[8:16, :], TAIL, 1)
        + pltpu.roll(tail_ref[16:24, :], 2 * TAIL, 1)
    )
    for i in range(2):
        own_ref[32 + i : 33 + i, 0:12] = slots_ref[i : i + 1, :].astype(jnp.float32)
    own_ref[34:35, :] = jnp.full((1, HEAD), count_ref[0, 0].astype(jnp.float32))
    pl.semaphore_wait(barrier, around - 1)

    def transfer(code):
        there, exists = place(OFFSETS[code])
        copy = pltpu.make_async_remote_copy(
            src_ref=own_ref,
            dst_ref=out_ref.at[26 - code],
            send_sem=send_sem.at[code],
            recv_sem=recv_sem.at[26 - code],
            device_id=there,
            device_id_type=pl.DeviceIdType.MESH,
        )
        return copy, exists

    for code in range(27):
        if code != 13:
            copy, exists = transfer(code)

            @pl.when(exists)
            def _():
                copy.start()

    out_ref[13] = own_ref[...]
    for code in range(27):
        if code != 13:
            there, exists = place(OFFSETS[code])

            @pl.when(jnp.logical_not(exists))
            def _():
                out_ref[code] = jnp.zeros(own_ref.shape, jnp.float32)

    for code in range(27):
        if code != 13:
            there, exists = place(OFFSETS[code])

            @pl.when(exists)
            def _():
                copy = pltpu.make_async_remote_copy(
                    src_ref=own_ref,
                    dst_ref=out_ref.at[code],
                    send_sem=send_sem.at[code],
                    recv_sem=recv_sem.at[code],
                    device_id=there,
                    device_id_type=pl.DeviceIdType.MESH,
                )
                copy.wait()

    for code in range(27):
        flat = out_ref[code, 32:MESSAGE, :].astype(jnp.int32)
        lanes = lax.broadcasted_iota(jnp.int32, (1, HEAD), 1)
        names_ref[code : code + 1, :] = jnp.where(
            lanes < 12, flat[0:1], jnp.where(lanes < 24, pltpu.roll(flat, 12, 1)[1:2], flat[2:3])
        )


def halo(shape, density, slots, count, sizes):
    vmem = pl.BlockSpec(memory_space=pltpu.VMEM)
    return pl.pallas_call(
        functools.partial(halo_kernel, sizes),
        out_shape=(
            jax.ShapeDtypeStruct((27, MESSAGE, HEAD), jnp.float32),
            jax.ShapeDtypeStruct((27, HEAD), jnp.int32),
        ),
        in_specs=[vmem, vmem, vmem, pl.BlockSpec(memory_space=pltpu.SMEM)],
        out_specs=(vmem, vmem),
        scratch_shapes=[
            pltpu.VMEM((MESSAGE, HEAD), jnp.float32),
            pltpu.VMEM((24, HEAD), jnp.float32),
            pltpu.SemaphoreType.DMA((27,)),
            pltpu.SemaphoreType.DMA((27,)),
        ],
        compiler_params=pltpu.CompilerParams(collective_id=0, has_side_effects=True),
        name="halo",
    )(shape, density, slots, count)


NT = (((1,), (1,)), ((), ()))


def split_three(value):
    first = value.astype(jnp.bfloat16).astype(jnp.float32)
    rest = value - first
    second = rest.astype(jnp.bfloat16).astype(jnp.float32)
    return first, second, rest - second


def near_kernel(
    names_ref, packed_hbm, source_hbm, target_table, analysis_ref, out_ref,
    coef, grids, centre, lifted, slab, totals, columns, target_list, source_list,
    packed_ref, source_table, copy_sem,
):
    delta2 = blob_radius * blob_radius
    packed_copy = pltpu.make_async_copy(packed_hbm, packed_ref, copy_sem.at[0])
    source_copy = pltpu.make_async_copy(source_hbm, source_table, copy_sem.at[1])
    packed_copy.start()
    source_copy.start()
    def scan_device(code, filled):
        def scan_slot(slot, filled):
            first = names_ref[code, slot]
            second = names_ref[code, 12 + slot]
            target_list[filled] = second & 3
            source_list[filled] = code * 4 + (first & 3)
            return filled + ((second >> 2) == 26 - code).astype(jnp.int32)

        return lax.fori_loop(0, names_ref[code, 24], scan_slot, filled)

    def own_slot(slot, filled):
        target_list[filled] = names_ref[13, slot] & 3
        source_list[filled] = names_ref[13, 12 + slot]
        return filled + 1

    filled = lax.fori_loop(0, 27, scan_device, 0)
    filled = lax.fori_loop(0, names_ref[13, 24], own_slot, filled)

    packed_copy.wait()
    lanes = lax.broadcasted_iota(jnp.int32, (27, 8, HEAD), 2)
    rows8 = lax.broadcasted_iota(jnp.int32, (27, 8, HEAD), 1)
    tails = packed_ref[:, 24:32, :]
    for group in range(3):
        head = packed_ref[:, 8 * group : 8 * group + 8, :]
        centre[:, 8 * group : 8 * group + 8, :] = jnp.broadcast_to(
            head[:, :, 0:1] * (0.5 / math.sqrt(math.pi)), head.shape
        )
        head = jnp.where((lanes == 0) & (rows8 + 8 * group < 12), 0.0, head)
        head_high = head.astype(jnp.bfloat16).astype(jnp.float32)
        tail = tails if group == 0 else pltpu.roll(tails, HEAD - TAIL * group, 2)
        tail = jnp.where(lanes < TAIL, tail, 0.0)
        tail_high = tail.astype(jnp.bfloat16).astype(jnp.float32)
        tail_low = tail - tail_high
        rows = slice(8 * group, 8 * group + 8)
        coef[:, rows, 0:128] = head_high
        coef[:, rows, 128:256] = head_high
        coef[:, rows, 256:384] = head - head_high
        coef[:, rows, 384:512] = (
            tail_high + pltpu.roll(tail_high, TAIL, 2) + pltpu.roll(tail_low, 2 * TAIL, 2)
        )

    own = coef[13].astype(jnp.bfloat16)
    row_points = lax.dot_general(own, target_table[...], NT, preferred_element_type=jnp.float32)

    slab[...] = jnp.zeros(slab.shape, jnp.float32)
    ones = jnp.ones((1, T_PAD), jnp.float32)
    for vesicle in range(4):
        x = [row_points[4 * i + vesicle : 4 * i + vesicle + 1, :] for i in range(3)]
        for i in range(3):
            slab[0, i : i + 1, 0:T_PAD] = x[i]
        slab[0, 3:4, 0:T_PAD] = ones
        slab[0, 4:5, 0:T_PAD] = x[0] * x[0] + x[1] * x[1] + x[2] * x[2] + delta2
        first, second, third = split_three(slab[0, :, 0:T_PAD])
        lifted[vesicle] = jnp.transpose(
            jnp.concatenate(
                [first, first, second, second, first, third]
                + [jnp.zeros((HEAD - 48, T_PAD), jnp.float32)]
            )
        ).astype(jnp.bfloat16)
    for copy in range(2):
        slab[copy, 4:5, :] = jnp.ones((1, S_PAD), jnp.float32)

    source_copy.wait()
    everything = coef[...].reshape(27 * 24, 512).astype(jnp.bfloat16)

    @pl.loop(0, S_PAD // CHUNK)
    def _(step):
        span = pl.ds(pl.multiple_of(step * CHUNK, CHUNK), CHUNK)
        grids[:, span] = jnp.dot(
            everything, source_table[:, span], preferred_element_type=jnp.float32
        )

    weight = jnp.concatenate(
        [analysis_ref[T_PAD + i : T_PAD + i + 1, :] for i in range(S_PAD // 256)], axis=1
    )
    totals[...] = jnp.zeros(totals.shape, jnp.float32)

    def process(item, columns, slab):
        target = target_list[item]
        entry = source_list[item]
        device = entry >> 2
        vesicle = entry & 3
        base = device * 24 + vesicle
        points, forces = [], []
        for i in range(3):
            moved = centre[device, pl.ds(4 * i + vesicle, 1), :] - centre[13, pl.ds(4 * i + target, 1), :]
            points.append(grids[pl.ds(base + 4 * i, 1), :] + jnp.concatenate([moved] * (S_PAD // HEAD), axis=1))
            forces.append(grids[pl.ds(base + 12 + 4 * i, 1), :] * weight)
        square = points[0] * points[0] + points[1] * points[1] + points[2] * points[2]
        for i in range(3):
            slab[i : i + 1, :] = -2.0 * points[i]
        slab[3:4, :] = square
        first, second, third = split_three(slab[...])
        right = jnp.concatenate([first, second, first, second, third, first]).astype(jnp.bfloat16)
        left = lifted[target, 0:T_ROWS, 0:48]
        square = square + 2.0 * delta2
        along = points[0] * forces[0] + points[1] * forces[1] + points[2] * forces[2]
        for i in range(3):
            columns[i : i + 1, :] = forces[i]
            for j in range(3):
                columns[3 + 3 * i + j : 4 + 3 * i + j, :] = forces[i] * points[j]
            columns[12 + i : 13 + i, :] = square * forces[i] + along * points[i]
        wide = columns[...]
        wide_high = wide.astype(jnp.bfloat16)
        wide_low = (wide - wide_high.astype(jnp.float32)).astype(jnp.bfloat16)
        both = jnp.concatenate([wide_high, wide_low], axis=0)
        parts, wides = [], []
        for step in range(S_PAD // CHUNK):
            span = slice(step * CHUNK, (step + 1) * CHUNK)
            softened = jnp.dot(left, right[:, span], preferred_element_type=jnp.float32)
            inverse = lax.rsqrt(softened)
            cube = inverse * inverse * inverse
            cube_high = cube.astype(jnp.bfloat16)
            cube_low = (cube - cube_high.astype(jnp.float32)).astype(jnp.bfloat16)
            parts += [cube_high, cube_low]
            wides += [both[:, span], both[:, span]]
        part = jnp.concatenate(parts, axis=1)
        wide = jnp.concatenate(wides, axis=1)
        total = lax.dot_general(part, wide, NT, preferred_element_type=jnp.float32)
        totals[target, 0:T_ROWS, 0 : 2 * COLS] += total

    @pl.loop(0, filled // 2)
    def _(item):
        process(2 * item, columns.at[0], slab.at[0])
        process(2 * item + 1, columns.at[1], slab.at[1])

    @pl.when(filled % 2 == 1)
    def _():
        process(filled - 1, columns.at[0], slab.at[0])

    for vesicle in range(4):
        turned = jnp.transpose(totals[vesicle])
        sums = turned[0:COLS] + turned[COLS : 2 * COLS]
        x = [row_points[4 * i + vesicle : 4 * i + vesicle + 1, :] for i in range(3)]
        plain = [sums[i : i + 1, :] for i in range(3)]
        cross = [[sums[3 + 3 * i + j : 4 + 3 * i + j, :] for j in range(3)] for i in range(3)]
        last = [sums[12 + i : 13 + i, :] for i in range(3)]
        square = x[0] * x[0] + x[1] * x[1] + x[2] * x[2]
        along = x[0] * plain[0] + x[1] * plain[1] + x[2] * plain[2]
        trace = cross[0][0] + cross[1][1] + cross[2][2]
        for i in range(3):
            value = square * plain[i] + x[i] * (along - trace) + last[i]
            for j in range(3):
                value = value - x[j] * (2.0 * cross[i][j] + cross[j][i])
            columns[0, 4 * i + vesicle : 4 * i + vesicle + 1, 0:T_PAD] = value * (0.125 / math.pi)
    result = jnp.dot(
        columns[0, :, 0:T_PAD],
        analysis_ref[0:T_PAD, :],
        precision=lax.Precision.HIGHEST,
        preferred_element_type=jnp.float32,
    )
    for i in range(3):
        out_ref[i] = result[4 * i : 4 * i + 4, 0 : HEAD + TAIL]


def near(names, packed, tables):
    vmem = pl.BlockSpec(memory_space=pltpu.VMEM)
    return pl.pallas_call(
        near_kernel,
        out_shape=jax.ShapeDtypeStruct((3, 4, HEAD + TAIL), jnp.float32),
        in_specs=[pl.BlockSpec(memory_space=pltpu.SMEM)] + [pl.BlockSpec(memory_space=pl.ANY)] * 2 + [vmem] * 2,
        out_specs=vmem,
        scratch_shapes=[
            pltpu.VMEM((27, 24, 512), jnp.float32),
            pltpu.VMEM((27 * 24, S_PAD), jnp.float32),
            pltpu.VMEM((27, 24, HEAD), jnp.float32),
            pltpu.VMEM((4, T_PAD, HEAD), jnp.bfloat16),
            pltpu.VMEM((2, 8, S_PAD), jnp.float32),
            pltpu.VMEM((4, T_PAD, HEAD), jnp.float32),
            pltpu.VMEM((2, COLS, S_PAD), jnp.float32),
            pltpu.SMEM((360,), jnp.int32),
            pltpu.SMEM((360,), jnp.int32),
            pltpu.VMEM((27, MESSAGE, HEAD), jnp.float32),
            pltpu.VMEM((512, S_PAD), jnp.bfloat16),
            pltpu.SemaphoreType.DMA((2,)),
        ],
        compiler_params=pltpu.CompilerParams(vmem_limit_bytes=48 * 1024 * 1024),
        name="near",
    )(names, packed, *tables)


def on_device(sizes, shape_coef, density_coef, pair_count, pair_slots):
    shape, density = (
        jnp.swapaxes(part[0, 0, 0], 0, 1) for part in (shape_coef, density_coef)
    )
    slots = pair_slots[0, 0, 0].T
    packed, names = halo(shape, density, slots, pair_count.reshape(1, 1), sizes)
    result = near(names, packed, grid_tables())
    return jnp.swapaxes(result, 0, 1)[None, None, None]


def solution(mesh):
    placed = (
        P("gx", "gy", "gz", None, None, None),
        P("gx", "gy", "gz", None, None, None),
        P("gx", "gy", "gz"),
        P("gx", "gy", "gz", None, None),
    )
    return jax.shard_map(
        functools.partial(on_device, tuple(mesh.shape[axis] for axis in AXES)),
        mesh=mesh,
        in_specs=placed,
        out_specs=P("gx", "gy", "gz", None, None, None),
        check_vma=False,
    )
```

profile of v0, /device:TPU:14, one launch (start us, length us, event | category | flops | bytes accessed | tf_op | source)
XLA Modules:
  0.0 44.8 jit_solution(16054439891859703019)
XLA Ops:
  0.7 9.9 %halo.1 = (f32[27,40,128]{2,1,0:T(8,128)}, s32[27,128]{1,0:T(8,128)}) custom-call(f32[3,4,169]{2,1,0:T(4,128)} %bitcast.14, f32[3,4,169]{2,1,0:T(4,128)} %bitcast.15, s32[2,12]{1,0:T(2,128)} %bitcast.16, s32[1,1]{1,0:T(1,128)} %bitcast.13.count_ref), custom_call_target="tpu_custom_call" | custom-call | tf_op jit(solution)/shard_map/halo/pallas_call | solution.py:228
  10.5 0.0 copy-start
  10.5 1.3 %copy-done = bf16[512,1280]{1,0:T(8,128)(2,1)S(1)} copy-done((bf16[512,1280]{1,0:T(8,128)(2,1)S(1)}, bf16[512,1280]{1,0:T(8,128)(2,1)}, u32[]{:S(2)}) %copy-start) | copy-done | bytes 1310744
  11.9 0.0 copy-start.1
  11.9 1.0 %copy-done.1 = f32[27,40,128]{2,1,0:T(8,128)S(1)} copy-done((f32[27,40,128]{2,1,0:T(8,128)S(1)}, f32[27,40,128]{2,1,0:T(8,128)}, u32[]{:S(2)}) %copy-start.1) | copy-done | bytes 552984
  12.9 0.0 copy-start.2
  12.9 1.0 %copy-done.2 = f32[392,256]{1,0:T(8,128)S(1)} copy-done((f32[392,256]{1,0:T(8,128)S(1)}, f32[392,256]{1,0:T(8,128)}, u32[]{:S(2)}) %copy-start.2) | copy-done | bytes 401432
  13.9 0.0 copy-start.3
  13.9 1.0 %copy-done.3 = bf16[384,512]{1,0:T(8,128)(2,1)S(1)} copy-done((bf16[384,512]{1,0:T(8,128)(2,1)S(1)}, bf16[384,512]{1,0:T(8,128)(2,1)}, u32[]{:S(2)}) %copy-start.3) | copy-done | bytes 393240
  14.9 0.0 copy-start.4
  14.9 0.7 %copy-done.4 = s32[27,128]{1,0:T(8,128)S(1)} copy-done((s32[27,128]{1,0:T(8,128)S(1)}, s32[27,128]{1,0:T(8,128)}, u32[]{:S(2)}) %copy-start.4) | copy-done | bytes 13848
  15.6 29.2 %near.1 = f32[3,4,169]{2,1,0:T(4,128)} custom-call(s32[27,128]{1,0:T(8,128)S(1)} %copy-done.4, f32[27,40,128]{2,1,0:T(8,128)S(1)} %copy-done.1, bf16[512,1280]{1,0:T(8,128)(2,1)S(1)} %copy-done, bf16[384,512]{1,0:T(8,128)(2,1)S(1)} %copy-done.3, f32[392,256]{1,0:T(8,128)S(1)} %copy-done.2), custom_call_target="tpu_custom_call" | custom-call | tf_op jit(solution)/shard_map/near/pallas_call | solution.py:424
Async XLA Ops:
  10.5 1.3 %copy-start = (bf16[512,1280]{1,0:T(8,128)(2,1)S(1)}, bf16[512,1280]{1,0:T(8,128)(2,1)}, u32[]{:S(2)}) copy-start(bf16[512,1280]{1,0:T(8,128)(2,1)} %constant.6.clone.source_hbm) | copy-start | bytes 3932164
  11.9 1.1 %copy-start.1 = (f32[27,40,128]{2,1,0:T(8,128)S(1)}, f32[27,40,128]{2,1,0:T(8,128)}, u32[]{:S(2)}) copy-start(f32[27,40,128]{2,1,0:T(8,128)} %get-tuple-element.8.packed_hbm) | copy-start | bytes 1658884
  12.9 1.0 %copy-start.2 = (f32[392,256]{1,0:T(8,128)S(1)}, f32[392,256]{1,0:T(8,128)}, u32[]{:S(2)}) copy-start(f32[392,256]{1,0:T(8,128)} %constant.8.clone.analysis_ref) | copy-start | bytes 1204228
  13.9 1.0 %copy-start.3 = (bf16[384,512]{1,0:T(8,128)(2,1)S(1)}, bf16[384,512]{1,0:T(8,128)(2,1)}, u32[]{:S(2)}) copy-start(bf16[384,512]{1,0:T(8,128)(2,1)} %constant.7.clone.target_table) | copy-start | bytes 1179652
  14.9 0.7 %copy-start.4 = (s32[27,128]{1,0:T(8,128)S(1)}, s32[27,128]{1,0:T(8,128)}, u32[]{:S(2)}) copy-start(s32[27,128]{1,0:T(8,128)} %get-tuple-element.7.names_ref) | copy-start | bytes 41476
where the time goes:
time: 44.1 us; the launch traced here: 44.8 us
  Pallas kernels  39.1 us (89%)
  local copies, waits for them, and re-layouts  5.07 us (11%)
  between operations  0.67 us (2%)
    pallas_call x1, Pallas kernels, near(): pl.pallas_call(near_kernel, out_shape=jax.ShapeDtypeStruct((3, 4, HEAD +...  29.2 us
    pallas_call x1, Pallas kernels, halo(): pl.pallas_call(functools.partial(halo_kernel, sizes), out_shape=(jax.Shap...  9.87 us
    unnamed x10, local copies, waits for them, and re-layouts  5.07 us

commit v1 on v0

--- a/solution.py
+++ b/solution.py
@@ -125,9 +125,23 @@
 
 
 def halo_kernel(
-    sizes, shape_ref, density_ref, slots_ref, count_ref, out_ref, names_ref,
-    own_ref, tail_ref, send_sem, recv_sem,
+    sizes, shape_hbm, density_hbm, slots_hbm, count_hbm, out_ref,
+    own_ref, tail_ref, blank_ref, shape_ref, density_ref, slots_ref, count_ref,
+    send_sem, recv_sem, local_sem,
 ):
+    loads = [
+        pltpu.make_async_copy(source, target, local_sem.at[27 + i])
+        for i, (source, target) in enumerate(
+            (
+                (shape_hbm, shape_ref),
+                (density_hbm, density_ref),
+                (slots_hbm, slots_ref),
+                (count_hbm, count_ref),
+            )
+        )
+    ]
+    for load in loads:
+        load.start()
     here = [lax.axis_index(axis) for axis in AXES]
 
     def place(offset):
@@ -153,8 +167,11 @@
                     barrier, inc=1, device_id=there, device_id_type=pl.DeviceIdType.MESH
                 )
 
+    blank_ref[...] = jnp.zeros(blank_ref.shape, jnp.float32)
     own_ref[32:MESSAGE, :] = jnp.zeros((MESSAGE - 32, HEAD), jnp.float32)
     tail_ref[...] = jnp.zeros(tail_ref.shape, jnp.float32)
+    for load in loads:
+        load.wait()
     for start, source in ((0, shape_ref), (12, density_ref)):
         for i in range(3):
             rows = slice(start + 4 * i, start + 4 * i + 4)
@@ -190,14 +207,27 @@
             def _():
                 copy.start()
 
-    out_ref[13] = own_ref[...]
+    def fill(code):
+        source = own_ref if code == 13 else blank_ref
+        return pltpu.make_async_copy(source, out_ref.at[code], local_sem.at[code])
+
+    fill(13).start()
     for code in range(27):
         if code != 13:
             there, exists = place(OFFSETS[code])
 
             @pl.when(jnp.logical_not(exists))
             def _():
-                out_ref[code] = jnp.zeros(own_ref.shape, jnp.float32)
+                fill(code).start()
+
+    fill(13).wait()
+    for code in range(27):
+        if code != 13:
+            there, exists = place(OFFSETS[code])
+
+            @pl.when(jnp.logical_not(exists))
+            def _():
+                fill(code).wait()
 
     for code in range(27):
         if code != 13:
@@ -215,29 +245,25 @@
                 )
                 copy.wait()
 
-    for code in range(27):
-        flat = out_ref[code, 32:MESSAGE, :].astype(jnp.int32)
-        lanes = lax.broadcasted_iota(jnp.int32, (1, HEAD), 1)
-        names_ref[code : code + 1, :] = jnp.where(
-            lanes < 12, flat[0:1], jnp.where(lanes < 24, pltpu.roll(flat, 12, 1)[1:2], flat[2:3])
-        )
-
 
 def halo(shape, density, slots, count, sizes):
-    vmem = pl.BlockSpec(memory_space=pltpu.VMEM)
+    hbm = pl.BlockSpec(memory_space=pltpu.HBM)
     return pl.pallas_call(
         functools.partial(halo_kernel, sizes),
-        out_shape=(
-            jax.ShapeDtypeStruct((27, MESSAGE, HEAD), jnp.float32),
-            jax.ShapeDtypeStruct((27, HEAD), jnp.int32),
-        ),
-        in_specs=[vmem, vmem, vmem, pl.BlockSpec(memory_space=pltpu.SMEM)],
-        out_specs=(vmem, vmem),
+        out_shape=jax.ShapeDtypeStruct((27, MESSAGE, HEAD), jnp.float32),
+        in_specs=[hbm] * 4,
+        out_specs=hbm,
         scratch_shapes=[
             pltpu.VMEM((MESSAGE, HEAD), jnp.float32),
             pltpu.VMEM((24, HEAD), jnp.float32),
+            pltpu.VMEM((MESSAGE, HEAD), jnp.float32),
+            pltpu.VMEM(shape.shape, jnp.float32),
+            pltpu.VMEM(density.shape, jnp.float32),
+            pltpu.VMEM(slots.shape, jnp.int32),
+            pltpu.SMEM(count.shape, jnp.int32),
             pltpu.SemaphoreType.DMA((27,)),
             pltpu.SemaphoreType.DMA((27,)),
+            pltpu.SemaphoreType.DMA((31,)),
         ],
         compiler_params=pltpu.CompilerParams(collective_id=0, has_side_effects=True),
         name="halo",
@@ -255,34 +281,33 @@
 
 
 def near_kernel(
-    names_ref, packed_hbm, source_hbm, target_table, analysis_ref, out_ref,
+    packed_hbm, source_hbm, target_hbm, analysis_hbm, out_ref,
     coef, grids, centre, lifted, slab, totals, columns, target_list, source_list,
-    packed_ref, source_table, copy_sem,
+    packed_ref, source_table, target_table, analysis_ref, flat_ref, names_ref, copy_sem,
 ):
     delta2 = blob_radius * blob_radius
-    packed_copy = pltpu.make_async_copy(packed_hbm, packed_ref, copy_sem.at[0])
-    source_copy = pltpu.make_async_copy(source_hbm, source_table, copy_sem.at[1])
-    packed_copy.start()
-    source_copy.start()
-    def scan_device(code, filled):
-        def scan_slot(slot, filled):
-            first = names_ref[code, slot]
-            second = names_ref[code, 12 + slot]
-            target_list[filled] = second & 3
-            source_list[filled] = code * 4 + (first & 3)
-            return filled + ((second >> 2) == 26 - code).astype(jnp.int32)
-
-        return lax.fori_loop(0, names_ref[code, 24], scan_slot, filled)
-
-    def own_slot(slot, filled):
-        target_list[filled] = names_ref[13, slot] & 3
-        source_list[filled] = names_ref[13, 12 + slot]
-        return filled + 1
-
-    filled = lax.fori_loop(0, 27, scan_device, 0)
-    filled = lax.fori_loop(0, names_ref[13, 24], own_slot, filled)
-
-    packed_copy.wait()
+    loads = [
+        pltpu.make_async_copy(source, target, copy_sem.at[i])
+        for i, (source, target) in enumerate(
+            (
+                (packed_hbm, packed_ref),
+                (target_hbm, target_table),
+                (source_hbm, source_table),
+                (analysis_hbm, analysis_ref),
+            )
+        )
+    ]
+    for load in loads:
+        load.start()
+    loads[0].wait()
+    lane = lax.broadcasted_iota(jnp.int32, (1, HEAD), 1)
+    for code in range(27):
+        flat = packed_ref[code, 32:MESSAGE, :].astype(jnp.int32)
+        flat_ref[code : code + 1, :] = jnp.where(
+            lane < 12, flat[0:1], jnp.where(lane < 24, pltpu.roll(flat, 12, 1)[1:2], flat[2:3])
+        )
+    names_copy = pltpu.make_async_copy(flat_ref, names_ref, copy_sem.at[4])
+    names_copy.start()
     lanes = lax.broadcasted_iota(jnp.int32, (27, 8, HEAD), 2)
     rows8 = lax.broadcasted_iota(jnp.int32, (27, 8, HEAD), 1)
     tails = packed_ref[:, 24:32, :]
@@ -306,6 +331,7 @@
         )
 
     own = coef[13].astype(jnp.bfloat16)
+    loads[1].wait()
     row_points = lax.dot_general(own, target_table[...], NT, preferred_element_type=jnp.float32)
 
     slab[...] = jnp.zeros(slab.shape, jnp.float32)
@@ -326,7 +352,7 @@
     for copy in range(2):
         slab[copy, 4:5, :] = jnp.ones((1, S_PAD), jnp.float32)
 
-    source_copy.wait()
+    loads[2].wait()
     everything = coef[...].reshape(27 * 24, 512).astype(jnp.bfloat16)
 
     @pl.loop(0, S_PAD // CHUNK)
@@ -336,6 +362,26 @@
             everything, source_table[:, span], preferred_element_type=jnp.float32
         )
 
+    names_copy.wait()
+    def scan_device(code, filled):
+        def scan_slot(slot, filled):
+            first = names_ref[code, slot]
+            second = names_ref[code, 12 + slot]
+            target_list[filled] = second & 3
+            source_list[filled] = code * 4 + (first & 3)
+            return filled + ((second >> 2) == 26 - code).astype(jnp.int32)
+
+        return lax.fori_loop(0, names_ref[code, 24], scan_slot, filled)
+
+    def own_slot(slot, filled):
+        target_list[filled] = names_ref[13, slot] & 3
+        source_list[filled] = names_ref[13, 12 + slot]
+        return filled + 1
+
+    filled = lax.fori_loop(0, 27, scan_device, 0)
+    filled = lax.fori_loop(0, names_ref[13, 24], own_slot, filled)
+
+    loads[3].wait()
     weight = jnp.concatenate(
         [analysis_ref[T_PAD + i : T_PAD + i + 1, :] for i in range(S_PAD // 256)], axis=1
     )
@@ -419,12 +465,12 @@
         out_ref[i] = result[4 * i : 4 * i + 4, 0 : HEAD + TAIL]
 
 
-def near(names, packed, tables):
+def near(packed, tables):
     vmem = pl.BlockSpec(memory_space=pltpu.VMEM)
     return pl.pallas_call(
         near_kernel,
         out_shape=jax.ShapeDtypeStruct((3, 4, HEAD + TAIL), jnp.float32),
-        in_specs=[pl.BlockSpec(memory_space=pltpu.SMEM)] + [pl.BlockSpec(memory_space=pl.ANY)] * 2 + [vmem] * 2,
+        in_specs=[pl.BlockSpec(memory_space=pltpu.HBM)] * 4,
         out_specs=vmem,
         scratch_shapes=[
             pltpu.VMEM((27, 24, 512), jnp.float32),
@@ -438,11 +484,15 @@
             pltpu.SMEM((360,), jnp.int32),
             pltpu.VMEM((27, MESSAGE, HEAD), jnp.float32),
             pltpu.VMEM((512, S_PAD), jnp.bfloat16),
-            pltpu.SemaphoreType.DMA((2,)),
+            pltpu.VMEM((T_PAD, 512), jnp.bfloat16),
+            pltpu.VMEM((T_PAD + 8, 256), jnp.float32),
+            pltpu.VMEM((32, HEAD), jnp.int32),
+            pltpu.SMEM((32, HEAD), jnp.int32),
+            pltpu.SemaphoreType.DMA((5,)),
         ],
-        compiler_params=pltpu.CompilerParams(vmem_limit_bytes=48 * 1024 * 1024),
+        compiler_params=pltpu.CompilerParams(vmem_limit_bytes=64 * 1024 * 1024),
         name="near",
-    )(names, packed, *tables)
+    )(packed, *tables)
 
 
 def on_device(sizes, shape_coef, density_coef, pair_count, pair_slots):
@@ -450,8 +500,8 @@
         jnp.swapaxes(part[0, 0, 0], 0, 1) for part in (shape_coef, density_coef)
     )
     slots = pair_slots[0, 0, 0].T
-    packed, names = halo(shape, density, slots, pair_count.reshape(1, 1), sizes)
-    result = near(names, packed, grid_tables())
+    packed = halo(shape, density, slots, pair_count.reshape(1, 1), sizes)
+    result = near(packed, grid_tables())
     return jnp.swapaxes(result, 0, 1)[None, None, None]
 
 

time: 44.1 us -> 34.4 us (0.78)
  the two profiles are of different devices: /device:TPU:14 before, /device:TPU:9 now
where the time goes in v1:
time: 34.4 us; the launch traced here: 34.9 us
  Pallas kernels  34.3 us (100%)
  between operations  0.66 us (2%)
    pallas_call x1, Pallas kernels, near(): pl.pallas_call(near_kernel, out_shape=jax.ShapeDtypeStruct((3, 4, HEAD +...  25.4 us
    pallas_call x1, Pallas kernels, halo(): pl.pallas_call(functools.partial(halo_kernel, sizes), out_shape=jax.Shape...  8.82 us

profile of v1, /device:TPU:9, one launch (start us, length us, event | category | flops | bytes accessed | tf_op | source)
XLA Modules:
  0.0 34.9 jit_solution(7135899156724948734)
XLA Ops:
  0.7 8.8 %halo.1.packed_hbm = f32[27,40,128]{2,1,0:T(8,128)} custom-call(f32[3,4,169]{2,1,0:T(4,128)} %bitcast.14, f32[3,4,169]{2,1,0:T(4,128)} %bitcast.15, s32[2,12]{1,0:T(2,128)} %bitcast.16, s32[1,1]{1,0:T(1,128)} %bitcast.13.count_hbm), custom_call_target="tpu_custom_call" | custom-call | tf_op jit(solution)/shard_map/halo/pallas_call | solution.py:251
  9.5 25.4 %near.1 = f32[3,4,169]{2,1,0:T(4,128)} custom-call(f32[27,40,128]{2,1,0:T(8,128)} %halo.1.packed_hbm, bf16[512,1280]{1,0:T(8,128)(2,1)} %constant.6.clone.source_hbm, bf16[384,512]{1,0:T(8,128)(2,1)} %constant.7.clone.target_hbm, f32[392,256]{1,0:T(8,128)} %constant.8.clone.analysis_hbm), custom_call_target="tpu_custom_call" | custom-call | tf_op jit(solution)/shard_map/near/pallas_call | solution.py:470

commit v2 on v1

--- a/solution.py
+++ b/solution.py
@@ -93,6 +93,7 @@
 T_ROWS = 352
 S_PAD = 1280
 CHUNK = 1280
+UNROLL = 4
 COLS = 16
 
 
@@ -168,7 +169,6 @@
                 )
 
     blank_ref[...] = jnp.zeros(blank_ref.shape, jnp.float32)
-    own_ref[32:MESSAGE, :] = jnp.zeros((MESSAGE - 32, HEAD), jnp.float32)
     tail_ref[...] = jnp.zeros(tail_ref.shape, jnp.float32)
     for load in loads:
         load.wait()
@@ -182,9 +182,10 @@
         + pltpu.roll(tail_ref[8:16, :], TAIL, 1)
         + pltpu.roll(tail_ref[16:24, :], 2 * TAIL, 1)
     )
+    names = jnp.full((1, HEAD), count_ref[0, 0].astype(jnp.float32))
+    own_ref[32:MESSAGE, :] = jnp.broadcast_to(names, (MESSAGE - 32, HEAD))
     for i in range(2):
-        own_ref[32 + i : 33 + i, 0:12] = slots_ref[i : i + 1, :].astype(jnp.float32)
-    own_ref[34:35, :] = jnp.full((1, HEAD), count_ref[0, 0].astype(jnp.float32))
+        own_ref[32:33, 12 * i : 12 * i + 12] = slots_ref[i : i + 1, :].astype(jnp.float32)
     pl.semaphore_wait(barrier, around - 1)
 
     def transfer(code):
@@ -300,12 +301,8 @@
     for load in loads:
         load.start()
     loads[0].wait()
-    lane = lax.broadcasted_iota(jnp.int32, (1, HEAD), 1)
     for code in range(27):
-        flat = packed_ref[code, 32:MESSAGE, :].astype(jnp.int32)
-        flat_ref[code : code + 1, :] = jnp.where(
-            lane < 12, flat[0:1], jnp.where(lane < 24, pltpu.roll(flat, 12, 1)[1:2], flat[2:3])
-        )
+        flat_ref[code : code + 1, :] = packed_ref[code, 32:33, :].astype(jnp.int32)
     names_copy = pltpu.make_async_copy(flat_ref, names_ref, copy_sem.at[4])
     names_copy.start()
     lanes = lax.broadcasted_iota(jnp.int32, (27, 8, HEAD), 2)
@@ -349,7 +346,7 @@
                 + [jnp.zeros((HEAD - 48, T_PAD), jnp.float32)]
             )
         ).astype(jnp.bfloat16)
-    for copy in range(2):
+    for copy in range(UNROLL):
         slab[copy, 4:5, :] = jnp.ones((1, S_PAD), jnp.float32)
 
     loads[2].wait()
@@ -431,10 +428,15 @@
         total = lax.dot_general(part, wide, NT, preferred_element_type=jnp.float32)
         totals[target, 0:T_ROWS, 0 : 2 * COLS] += total
 
-    @pl.loop(0, filled // 2)
+    @pl.loop(0, filled // UNROLL)
     def _(item):
-        process(2 * item, columns.at[0], slab.at[0])
-        process(2 * item + 1, columns.at[1], slab.at[1])
+        for copy in range(UNROLL):
+            process(UNROLL * item + copy, columns.at[copy], slab.at[copy])
+
+    @pl.when(filled % 4 >= 2)
+    def _():
+        for copy in range(2):
+            process(filled // 4 * 4 + copy, columns.at[copy], slab.at[copy])
 
     @pl.when(filled % 2 == 1)
     def _():
@@ -477,9 +479,9 @@
             pltpu.VMEM((27 * 24, S_PAD), jnp.float32),
             pltpu.VMEM((27, 24, HEAD), jnp.float32),
             pltpu.VMEM((4, T_PAD, HEAD), jnp.bfloat16),
-            pltpu.VMEM((2, 8, S_PAD), jnp.float32),
+            pltpu.VMEM((UNROLL, 8, S_PAD), jnp.float32),
             pltpu.VMEM((4, T_PAD, HEAD), jnp.float32),
-            pltpu.VMEM((2, COLS, S_PAD), jnp.float32),
+            pltpu.VMEM((UNROLL, COLS, S_PAD), jnp.float32),
             pltpu.SMEM((360,), jnp.int32),
             pltpu.SMEM((360,), jnp.int32),
             pltpu.VMEM((27, MESSAGE, HEAD), jnp.float32),

time: 34.4 us -> 34.6 us (level)
  the two profiles are of different devices: /device:TPU:9 before, /device:TPU:18 now
where the time goes in v2:
time: 34.6 us; the launch traced here: 34.3 us
  Pallas kernels  33.6 us (97%)
  between operations  0.66 us (2%)
    pallas_call x1, Pallas kernels, near(): pl.pallas_call(near_kernel, out_shape=jax.ShapeDtypeStruct((3, 4, HEAD +...  25.7 us
    pallas_call x1, Pallas kernels, halo(): pl.pallas_call(functools.partial(halo_kernel, sizes), out_shape=jax.Shape...  7.92 us

profile of v2, /device:TPU:18, one launch (start us, length us, event | category | flops | bytes accessed | tf_op | source)
XLA Modules:
  0.0 34.3 jit_solution(10050583400875773757)
XLA Ops:
  0.7 7.9 %halo.1.packed_hbm = f32[27,40,128]{2,1,0:T(8,128)} custom-call(f32[3,4,169]{2,1,0:T(4,128)} %bitcast.14, f32[3,4,169]{2,1,0:T(4,128)} %bitcast.15, s32[2,12]{1,0:T(2,128)} %bitcast.16, s32[1,1]{1,0:T(1,128)} %bitcast.13.count_hbm), custom_call_target="tpu_custom_call" | custom-call | tf_op jit(solution)/shard_map/halo/pallas_call | solution.py:252
  8.6 25.7 %near.1 = f32[3,4,169]{2,1,0:T(4,128)} custom-call(f32[27,40,128]{2,1,0:T(8,128)} %halo.1.packed_hbm, bf16[512,1280]{1,0:T(8,128)(2,1)} %constant.6.clone.source_hbm, bf16[384,512]{1,0:T(8,128)(2,1)} %constant.7.clone.target_hbm, f32[392,256]{1,0:T(8,128)} %constant.8.clone.analysis_hbm), custom_call_target="tpu_custom_call" | custom-call | tf_op jit(solution)/shard_map/near/pallas_call | solution.py:472
